TPU v7x, 32 devices: a whole 2x2x4 slice. The times are simulated.
32 devices in a mesh: dp: 4 (over y, x), space: 8 (over z, core).
Axes of the slice: x: 2, y: 2, z: 4, core: 2. Of those that a mesh axis runs over, the one named last changes fastest.
Arguments:
- image: bfloat16 [4, 64, 10240], P('dp', 'space'), may hold values from -6 to 6
- cotangent: bfloat16 [4, 32, 5120], P('dp', 'space'), may hold values from -6 to 6
- weight: float32 [1440, 160], P('dp'), may hold values from -0.15625 to 0.15625
- moment_one: float32 [1440, 160], P('dp'), may hold values from -0.25 to 0.25
- moment_two: float32 [1440, 160], P('dp'), may hold values from 6.1035156e-05 to 0.0009765625
Outputs:
- output: bfloat16 [4, 32, 5120], P('dp', 'space')
- grad_image: bfloat16 [4, 64, 10240], P('dp', 'space')
- new_weight: float32 [1440, 160], P('dp')
- new_moment_one: float32 [1440, 160], P('dp')
- new_moment_two: float32 [1440, 160], P('dp')
All inputs are finite; a program needn't handle non-finite values.
Results may differ from a plain program's by a relative error of at most 0.0049.
Values may be sent and summed in bfloat16 or wider, within the bound.
A program may use at most 64 MiB of HBM per device.

v0:
```python
import jax
import jax.numpy as jnp
from jax import lax
from jax.sharding import PartitionSpec as P

beta_one = 0.9
beta_two = 0.999
learn_rate = 0.01
decay_rate = 0.01
epsilon = 1e-08
adam_step = 10


def from_behind(block, axis, distance):
    devices = range(lax.axis_size(axis))
    route = [(i - distance, i) for i in devices if i - distance in devices]
    return lax.ppermute(block, axis, route)


def body(image, cotangent, weight, moment_one, moment_two):
    channels = weight.shape[1]
    samples, rows_here, merged = image.shape
    cols_here = merged // channels
    out_rows = rows_here // 2
    out_cols = cols_here // 2
    positions = samples * out_rows * out_cols
    above_flat = from_behind(image[:, rows_here - 1 : rows_here], "space", 1)
    above_row = above_flat.reshape(samples, 1, cols_here, channels)
    image_four = image.reshape(samples, rows_here, cols_here, channels)
    padded = jnp.concatenate([above_row, image_four], axis=1)
    padded = jnp.pad(padded, ((0, 0), (0, 0), (1, 1), (0, 0)))
    pieces = [
        padded[
            :, row_tap : row_tap + 2 * out_rows - 1 : 2, col_tap : col_tap + 2 * out_cols - 1 : 2, :
        ]
        for row_tap in range(3)
        for col_tap in range(3)
    ]
    patches = jnp.concatenate(pieces, axis=3).reshape(positions, 9 * channels)
    kernel_half = weight.astype(jnp.bfloat16)
    forward = jnp.dot(
        patches,
        lax.all_gather(kernel_half, "dp", axis=0, tiled=True),
        preferred_element_type=jnp.float32,
    )
    output = forward.astype(jnp.bfloat16).reshape(samples, out_rows, out_cols * channels)
    used_rows = cotangent.shape[1]
    cotan_flat = cotangent.reshape(samples * used_rows * out_cols, channels)
    patch_grads = lax.dot_general(
        cotan_flat,
        lax.all_gather(kernel_half, "dp", axis=0, tiled=True),
        (((1,), (1,)), ((), ())),
        preferred_element_type=jnp.float32,
    )
    patch_grads = patch_grads.reshape(samples, used_rows, out_cols, 3, 3, channels)
    even_cols = patch_grads[:, :, :, :, 1, :]
    left_taps = patch_grads[:, :, :, :, 0, :]
    left_next = jnp.concatenate([left_taps[:, :, 1:], jnp.zeros_like(left_taps[:, :, 0:1])], axis=2)
    odd_cols = patch_grads[:, :, :, :, 2, :] + left_next
    by_column = jnp.stack([even_cols, odd_cols], axis=3).reshape(
        samples, used_rows, cols_here, 3, channels
    )
    even_rows = by_column[:, 0:out_rows, :, 1, :]
    upper_taps = by_column[:, :, :, 0, :]
    upper_next = jnp.concatenate(
        [upper_taps[:, 1:out_rows], jnp.zeros_like(upper_taps[:, 0:1])], axis=1
    )
    odd_rows = by_column[:, 0:out_rows, :, 2, :] + upper_next
    edge_flat = upper_taps[:, 0:1].reshape(samples, 1, cols_here * channels)
    sent_edge = from_behind(edge_flat, "space", -1)
    odd_rows = odd_rows.at[:, out_rows - 1 : out_rows].add(
        sent_edge.reshape(samples, 1, cols_here, channels)
    )
    grad_image = (
        jnp.stack([even_rows, odd_rows], axis=2)
        .reshape(samples, rows_here, cols_here * channels)
        .astype(jnp.bfloat16)
    )
    grad_flat = cotangent.reshape(positions, channels)
    full_grad = lax.dot_general(
        patches, grad_flat, (((0,), (0,)), ((), ())), preferred_element_type=jnp.float32
    )
    by_cols = lax.psum_scatter(
        full_grad.astype(jnp.bfloat16), "space", scatter_dimension=1, tiled=True
    ).astype(jnp.float32)
    by_owner = lax.psum_scatter(by_cols, "dp", scatter_dimension=0, tiled=True)
    grad_shard = lax.all_gather(by_owner, "space", axis=1, tiled=True)
    total_count = positions * lax.axis_size("dp") * lax.axis_size("space")
    gradient = grad_shard / float(total_count)
    new_moment_one = beta_one * moment_one + (1.0 - beta_one) * gradient
    new_moment_two = beta_two * moment_two + (1.0 - beta_two) * gradient * gradient
    first_hat = new_moment_one / (1.0 - beta_one**adam_step)
    second_hat = new_moment_two / (1.0 - beta_two**adam_step)
    new_weight = weight - learn_rate * (
        first_hat / (jnp.sqrt(second_hat) + epsilon) + decay_rate * weight
    )
    return (output, grad_image, new_weight, new_moment_one, new_moment_two)


def solution(mesh):
    in_specs = (
        P("dp", "space", None),
        P("dp", "space", None),
        P("dp", None),
        P("dp", None),
        P("dp", None),
    )
    out_specs = (
        P("dp", "space", None),
        P("dp", "space", None),
        P("dp", None),
        P("dp", None),
        P("dp", None),
    )
    return jax.shard_map(body, mesh=mesh, in_specs=in_specs, out_specs=out_specs, check_vma=False)
```

profile of v0, /device:TPU:0, one launch (start us, length us, event | category | flops | bytes accessed | tf_op | source)
XLA Modules:
  0.0 129.7 jit_solution(1042519516029350568)
XLA Ops:
  7.2 1.0 slice.87
  8.2 2.4 %collective-permute-start = (bf16[1,1,10240]{2,1,0:T(2,128)(2,1)S(1)}, bf16[1,1,10240]{2,1,0:T(2,128)(2,1)S(1)}, u32[]{:S(2)}, u32[]{:S(2)}) collective-permute-start(bf16[1,1,10240]{2,1,0:T(2,128)(2,1)S(1)} %slice.87), channel_id=1, source_target_pairs={{0,1},{1,2},{2,3},{3,4},{4,5},{5,6},{6,7},{8,9},{9,10},{10,11},{11... | collective-permute-start | bytes 61448 | tf_op jit(solution)/shard_map/ppermute | solution.py:17
  10.5 1.2 reshape.97
  11.8 0.9 reshape.104
  15.6 22.9 %fusion = bf16[1440,24]{0,1:T(8,128)(2,1)S(1)} fusion(bf16[1440,160]{0,1:T(8,128)(2,1)S(1)} %convolution_convert_fusion), kind=kCustom, calls=%all-reduce-scatter | all-reduce-scatter fusion | flops 276481 | bytes 530432
  38.5 1.3 collective-permute-start.2
  39.8 1.3 collective-permute-start.3
  41.1 0.6 dynamic-slice.13
  42.9 0.7 dynamic-slice_convert_fusion
  43.8 0.6 dynamic-slice.9
  45.0 41.8 %all-reduce.8.cloned.1.call-done = f32[1440,20]{0,1:T(8,128)} async-done(((f32[1440,20]{0,1:T(8,128)}), f32[1440,20]{0,1:T(8,128)}) %all-reduce.8.cloned.1.call-update) | async-done | bytes 115216
  86.8 0.9 dynamic-slice_bitcast_fusion
  87.7 14.3 %all-gather.1 = f32[8,20,360]{2,1,0:T(8,128)S(1)} all-gather(f32[1,20,360]{2,1,0:T(8,128)S(1)} %dynamic-slice_bitcast_fusion), channel_id=1, replica_groups=mesh['dp'=4,'space'=8] {'space'}, dimensions={0}, use_global_device_ids=true | all-gather | bytes 259200 | tf_op jit(solution)/shard_map/all_gather | solution.py:87
  102.2 1.0 multiply_subtract_fusion
  103.1 10.0 %all-gather = bf16[4,360,160]{1,2,0:T(8,128)(2,1)S(1)} all-gather(bf16[1,360,160]{1,2,0:T(8,128)(2,1)S(1)} %get-tuple-element.26), channel_id=1, replica_groups=mesh['dp'=4,'space'=8] {'dp'}, dimensions={0}, use_global_device_ids=true | all-gather | bytes 576000 | tf_op jit(solution)/shard_map/all_gather | solution.py:43
  113.7 0.4 convolution_bitcast_fusion
  114.3 0.5 copy.37
  115.9 1.3 collective-permute-start.1
  117.4 0.8 reshape.99
  118.2 0.8 collective-permute-done.1
  119.0 0.5 broadcast.64
  119.5 0.7 reduce.8
  120.5 1.0 scatter-add.4
  121.8 1.0 convert_element_type.28
  (57 shorter events, 6.2 us)
Async XLA Ops:
  7.2 79.7 %all-reduce.8.cloned.1.call-start = ((), (), s32[]{:S(2)}) async-start(), calls=%async_computation | async-start | bytes 294912
  8.2 4.5 %collective-permute-start = (bf16[1,1,10240]{2,1,0:T(2,128)(2,1)S(1)}, bf16[1,1,10240]{2,1,0:T(2,128)(2,1)S(1)}, u32[]{:S(2)}, u32[]{:S(2)}) collective-permute-start(bf16[1,1,10240]{2,1,0:T(2,128)(2,1)S(1)} %slice.87), channel_id=1, source_target_pairs={{0,1},{1,2},{2,3},{3,4},{4,5},{5,6},{6,7},{8,9},{9,10},{10,11},{11... | collective-permute-start | bytes 61448 | tf_op jit(solution)/shard_map/ppermute | solution.py:17
  15.0 26.1 %copy-start.4 = (u32[32]{0:T(128)S(1)}, u32[32]{0:T(128)}, u32[]{:S(2)}) copy-start(u32[32]{0:T(128)} %constant.69) | copy-start | bytes 388
  15.3 28.3 %copy-start.3 = (bf16[1,4,5120]{2,1,0:T(4,128)(2,1)S(1)}, bf16[1,4,5120]{2,1,0:T(4,128)(2,1)}, u32[]{:S(2)}) copy-start(bf16[1,4,5120]{2,1,0:T(4,128)(2,1)} %param.8) | copy-start | bytes 122884
  15.3 28.5 %copy-start.5 = (u32[32]{0:T(128)S(1)}, u32[32]{0:T(128)}, u32[]{:S(2)}) copy-start(u32[32]{0:T(128)} %constant.73) | copy-start | bytes 388
  38.5 4.0 %collective-permute-start.2 = (bf16[1440,24]{0,1:T(8,128)(2,1)S(1)}, bf16[1440,24]{0,1:T(8,128)(2,1)S(1)}, u32[]{:S(2)}, u32[]{:S(2)}) collective-permute-start(bf16[1440,24]{0,1:T(8,128)(2,1)S(1)} %fusion), channel_id=1, source_target_pairs={{0,1},{1,2},{2,3},{3,4},{4,5},{5,6},{6,7},{8,9},{9,10},{10,11},{11... | collective-permute-start | bytes 207368
  39.8 2.7 %collective-permute-start.3 = (bf16[1440,4]{0,1:T(4,128)(2,1)S(1)}, bf16[1440,4]{0,1:T(4,128)(2,1)S(1)}, u32[]{:S(2)}, u32[]{:S(2)}) collective-permute-start(bf16[1440,4]{0,1:T(4,128)(2,1)S(1)} %slice.117), channel_id=1, source_target_pairs={{0,2},{1,3},{2,4},{3,5},{4,6},{5,7},{8,10},{9,11},{10,12},{11,13},... | collective-permute-start | bytes 34568
  45.0 57.1 %copy-start = (f32[360,160]{0,1:T(8,128)S(1)}, f32[360,160]{0,1:T(8,128)}, u32[]{:S(2)}) copy-start(f32[360,160]{0,1:T(8,128)} %param.9) | copy-start | bytes 691204
  45.0 57.1 %copy-start.1 = (f32[360,160]{0,1:T(8,128)S(1)}, f32[360,160]{0,1:T(8,128)}, u32[]{:S(2)}) copy-start(f32[360,160]{0,1:T(8,128)} %param.10) | copy-start | bytes 691204
  45.0 57.1 %copy-start.2 = (f32[360,160]{0,1:T(8,128)S(1)}, f32[360,160]{0,1:T(8,128)}, u32[]{:S(2)}) copy-start(f32[360,160]{0,1:T(8,128)} %param.11) | copy-start | bytes 691204
  115.9 3.1 %collective-permute-start.1 = (f32[1,1,10240]{2,1,0:T(1,128)S(1)}, f32[1,1,10240]{2,1,0:T(1,128)S(1)}, u32[]{:S(2)}, u32[]{:S(2)}) collective-permute-start(f32[1,1,10240]{2,1,0:T(1,128)S(1)} %reshape.102), channel_id=1, source_target_pairs={{1,0},{2,1},{3,2},{4,3},{5,4},{6,5},{7,6},{9,8},{10,9},{11,10},{12... | collective-permute-start | bytes 122888 | tf_op jit(solution)/shard_map/ppermute | solution.py:17
Sparse Core Ops, SparseCore 0:
  43.7 43.0 all-reduce.7
where the time goes:
time: 132 us; the launch traced here: 130 us
  blocking collectives  47.2 us (36%)
  waiting for transfers between devices  42.7 us (32%)
  between operations  15.8 us (12%)
  local copies, waits for them, and re-layouts  13.5 us (10%)
  starting transfers between devices  6.27 us (5%)
  other arithmetic  3.21 us (2%)
    unnamed x4, waiting for transfers between devices  41.9 us
    unnamed x1, blocking collectives  22.9 us
    all_gather x1, blocking collectives, body(): grad_shard = lax.all_gather(by_owner, 'space', axis=1, tiled=True)  14.3 us
    all_gather x1, blocking collectives, body(): lax.all_gather(kernel_half, 'dp', axis=0, tiled=True)  10 us
    ppermute x2, starting transfers between devices, from_behind(): return lax.ppermute(block, axis, route)  3.65 us
    unnamed x18, local copies, waits for them, and re-layouts  2.83 us
  transfers between devices with their start and end apart: 5, of which 3 were waited for; matrix products, arithmetic and copies ran while one was open for 3% of the time, Pallas kernels for 0%

commit v1 on v0

v1 whole, which is shorter than its diff:
```python
import functools

import jax
import jax.numpy as jnp
from jax import lax
from jax.experimental import pallas as pl
from jax.experimental.pallas import tpu as pltpu
from jax.sharding import PartitionSpec as P

MESH = pl.DeviceIdType.MESH
F32 = jnp.float32
BF16 = jnp.bfloat16

beta_one = 0.9
beta_two = 0.999
learn_rate = 0.01
decay_rate = 0.01
epsilon = 1e-08
adam_step = 10


def up(value, unit):
    return -(-value // unit) * unit


def kernel(
    n_dp, n_space, count,
    image, cotangent, weight, moment_one, moment_two,
    out, grad_image, new_weight, new_one, new_two,
    even, odd, cot, cot_next, img_edge_out, img_edge_in, cot_edge_out, cot_edge_in,
    wt, taps, part, mate_out, mate_in, own, dp_out, dp_in, shares, z_out, z_in, final, total,
    edge_send, edge_recv, w_send, w_recv, wm_send, wm_recv, m_send, m_recv,
    d_send, d_recv, z_send, z_recv, f_send, f_recv,
):
    C = weight.shape[1]
    half = C // 2
    rest = C - 128
    shard = weight.shape[0]
    wide = wt.shape[-1]
    cols = out.shape[2] // C
    out_rows = out.shape[1]
    rows = image.shape[1]
    positions = cols * out_rows
    nz = n_space // 2
    sub = wide // nz
    dp = lax.axis_index("dp")
    space = lax.axis_index("space")
    core = lax.rem(space, 2)
    zi = lax.div(space, 2)
    mate = space + 1 - 2 * core

    barrier = pltpu.get_barrier_semaphore()
    for k in range(1, n_dp):
        pl.semaphore_signal(barrier, inc=1, device_id=(lax.rem(dp + k, n_dp), space), device_id_type=MESH)
    for k in range(1, n_space):
        pl.semaphore_signal(barrier, inc=1, device_id=(dp, lax.rem(space + k, n_space)), device_id_type=MESH)

    def remote(src, dst, send, recv, to_dp, to_space):
        return pltpu.make_async_remote_copy(
            src_ref=src, dst_ref=dst, send_sem=send, recv_sem=recv,
            device_id=(to_dp, to_space), device_id_type=MESH)

    zeros_e = jnp.zeros(even.shape[1:], F32)
    even[1] = zeros_e
    odd[1] = zeros_e
    odd[0, 0:16, :] = jnp.zeros((16, 128), F32)
    cot[1] = jnp.zeros(cot.shape[1:], F32)
    cot[0, pl.ds(positions, 8), :] = jnp.zeros((8, 128), F32)
    cot_next[0, pl.ds(positions, 8), :] = jnp.zeros((8, 128), F32)
    cot_next[1, pl.ds(positions, 8), :] = jnp.zeros((8, 128), F32)

    group = 4 * C

    def split_cot(g, carry):
        v = cotangent[0, :, pl.ds(pl.multiple_of(g * group, 128), group)].astype(F32)
        pieces = [v[:, k * C : (k + 1) * C] for k in range(4)]
        for k in range(0, 4, 2):
            both = jnp.concatenate([pieces[k], pieces[k + 1]], axis=0)
            at = pl.multiple_of((4 * g + k) * out_rows, 8)
            cot[0, pl.ds(at, 8), :] = both[:, :128]
            cot[1, pl.ds(at, 8), 0:rest] = both[:, 128:]
        return carry

    lax.fori_loop(0, cols // 4, split_cot, 0)

    def split_image(g, carry):
        v = image[0, :, pl.ds(pl.multiple_of(g * group, 128), group)].astype(F32)
        for k in range(4):
            piece = v[:, k * C : (k + 1) * C]
            ref = odd if k % 2 else even
            at = pl.multiple_of((2 * g + k // 2) * rows + 16, 8)
            ref[0, pl.ds(at, rows), :] = piece[:, :128]
            ref[1, pl.ds(at, rows), 0:rest] = piece[:, 128:]
        return carry

    lax.fori_loop(0, cols // 2, split_image, 0)

    def strided(ref, start, size, stride):
        at = pl.ds(start, size, stride=stride)
        return jnp.concatenate([ref[0, at, :], ref[1, at, :]], axis=1)[:, :C]

    img_edge_out[0:cols] = strided(even, 16 + rows - 1, cols, rows).astype(BF16)
    img_edge_out[cols : 2 * cols] = strided(odd, 16 + rows - 1, cols, rows).astype(BF16)
    cot_edge_out[...] = strided(cot, 0, cols, out_rows).astype(BF16)

    eye = (lax.broadcasted_iota(jnp.int32, (C, C), 0) == lax.broadcasted_iota(jnp.int32, (C, C), 1))
    eye = eye.astype(F32).astype(BF16)
    mine = lax.dot_general(eye, weight[...].astype(BF16), (((1,), (1,)), ((), ())),
                           preferred_element_type=F32).astype(BF16)
    wt[dp, 0, :, 0:shard] = mine[:half]
    wt[dp, 1, :, 0:shard] = mine[half:]

    pl.semaphore_wait(barrier, n_dp + n_space - 2)

    img_copy = remote(img_edge_out, img_edge_in, edge_send.at[0], edge_recv.at[0], dp, lax.rem(space + 1, n_space))
    cot_copy = remote(cot_edge_out, cot_edge_in, edge_send.at[1], edge_recv.at[1], dp, lax.rem(space + n_space - 1, n_space))

    img_copy.start()
    cot_copy.start()

    def w_copy(k):
        return remote(wt.at[dp, core], wt.at[dp, core], w_send.at[k], w_recv.at[k], lax.rem(dp + k, n_dp), space)

    for k in range(1, n_dp):
        w_copy(k).start()

    whole_cot = strided(cot, 0, positions, 1)
    cot_t = whole_cot.T.astype(BF16)
    first, second = cot_t[:half], cot_t[half:]
    lower = core == 0
    mate_rows = jnp.where(lower, second.astype(F32), first.astype(F32)).astype(BF16)
    own_rows = jnp.where(lower, first.astype(F32), second.astype(F32)).astype(BF16)

    def patch(r, s):
        ref = even if s == 1 else odd
        start = 16 + r - 1 - (rows if s == 0 else 0)
        return strided(ref, start, positions, 2).astype(BF16)

    def place(ref, tap, value, by_shard):
        lo = tap * C
        end = lo + C
        while lo < end:
            d = lo // shard
            stop = min(end, (d + 1) * shard)
            ref[d, :, lo - d * shard : stop - d * shard] = value[:, lo - tap * C : stop - tap * C]
            lo = stop

    for d in range(n_dp):
        if wide > shard:
            pad = jnp.zeros((half, wide - shard), F32)
            own[d, :, shard:wide] = pad
            part[d, :, shard:wide] = pad

    def grads(r):
        for s in range(3):
            p = patch(r, s)
            taps[3 * r + s] = p
            place(part, 3 * r + s, jnp.dot(mate_rows, p, preferred_element_type=F32), True)

    grads(1)
    grads(2)
    img_copy.wait()

    @pl.when(space == 0)
    def _():
        img_edge_in[...] = jnp.zeros(img_edge_in.shape, BF16)

    for base, ref in ((0, even), (cols, odd)):
        edge = img_edge_in[base : base + cols].astype(F32)
        at = pl.ds(15, cols, stride=rows)
        ref[0, at, :] = edge[:, :128]
        ref[1, at, :] = jnp.concatenate([edge[:, 128:], jnp.zeros((cols, 256 - C), F32)], axis=1)
    grads(0)
    mate_out[...] = part[...].astype(BF16)
    mate_copy = remote(mate_out, mate_in, m_send.at[0], m_recv.at[0], dp, mate)
    mate_copy.start()

    def wm_copy(k):
        src = lax.rem(dp + n_dp - k, n_dp)
        return remote(wt.at[src, core], wt.at[src, core], wm_send.at[k], wm_recv.at[k], dp, mate)

    for k in range(1, n_dp):
        w_copy(k).wait()
        wm_copy(k).start()

    for t in range(9):
        place(own, t, jnp.dot(own_rows, taps[t], preferred_element_type=F32), True)

    mate_copy.wait()
    own[...] = own[...] + mate_in[...].astype(F32)

    dp_out[...] = own[...].astype(BF16)

    def d_copy(k):
        to = lax.rem(dp + k, n_dp)
        return remote(dp_out.at[to], dp_in.at[k], d_send.at[k], d_recv.at[k], to, space)

    for k in range(1, n_dp):
        d_copy(k).start()

    for k in range(1, n_dp):
        wm_copy(k).wait()

    def tap_t(t):
        lo = t * C
        end = lo + C
        pieces = []
        while lo < end:
            d = lo // shard
            stop = min(end, (d + 1) * shard)
            at = slice(lo - d * shard, stop - d * shard)
            pieces.append(jnp.concatenate([wt[d, 0, :, at], wt[d, 1, :, at]], axis=0).astype(F32))
            lo = stop
        value = pieces[0] if len(pieces) == 1 else jnp.concatenate(pieces, axis=1)
        return value.astype(BF16)

    kern = [tap_t(t) for t in range(9)]
    acc = jnp.zeros((positions, C), F32)
    for t in range(9):
        acc = acc + lax.dot_general(taps[t], kern[t], (((1,), (1,)), ((), ())), preferred_element_type=F32)
    total_shape = total.shape

    def keep(ref, at, value):
        ref[0, at, :] = value[:, :128]
        ref[1, at, :] = jnp.concatenate([value[:, 128:], jnp.zeros((value.shape[0], 256 - C), F32)], axis=1)

    keep(even, pl.ds(0, positions), acc)

    def join_out(g, carry):
        pieces = []
        for k in range(0, 4, 2):
            at = pl.multiple_of((4 * g + k) * out_rows, 8)
            v = jnp.concatenate([even[0, pl.ds(at, 8), :], even[1, pl.ds(at, 8), 0:rest]], axis=1)
            pieces += [v[:out_rows], v[out_rows:]]
        out[0, :, pl.ds(pl.multiple_of(g * group, 128), group)] = jnp.concatenate(pieces, axis=1).astype(BF16)
        return carry

    lax.fori_loop(0, cols // 4, join_out, 0)

    cot_copy.wait()

    @pl.when(space == n_space - 1)
    def _():
        cot_edge_in[...] = jnp.zeros(cot_edge_in.shape, BF16)

    for h in range(2):
        cot_next[h, pl.ds(0, positions), :] = cot[h, pl.ds(1, positions), :]
    edge = cot_edge_in[...].astype(F32)
    at = pl.ds(out_rows - 1, cols, stride=out_rows)
    keep(cot_next, at, edge)
    here = whole_cot.astype(BF16)
    right = strided(cot, out_rows, positions, 1).astype(BF16)
    below = strided(cot_next, 0, positions, 1).astype(BF16)
    both = strided(cot_next, out_rows, positions, 1).astype(BF16)

    def back(c, r, s):
        return jnp.dot(c, kern[3 * r + s], preferred_element_type=F32)

    keep(even, pl.ds(0, positions, stride=2), back(here, 1, 1))
    keep(even, pl.ds(1, positions, stride=2), back(here, 2, 1) + back(below, 0, 1))
    keep(odd, pl.ds(0, positions, stride=2), back(here, 1, 2) + back(right, 1, 0))
    keep(odd, pl.ds(1, positions, stride=2),
         back(here, 2, 2) + back(right, 2, 0) + back(below, 0, 2) + back(both, 0, 0))

    def join_grad(g, carry):
        pieces = []
        for k in range(4):
            ref = odd if k % 2 else even
            at = pl.multiple_of((2 * g + k // 2) * rows, 8)
            pieces.append(jnp.concatenate([ref[0, pl.ds(at, rows), :], ref[1, pl.ds(at, rows), 0:rest]], axis=1))
        grad_image[0, :, pl.ds(pl.multiple_of(g * group, 128), group)] = jnp.concatenate(pieces, axis=1).astype(BF16)
        return carry

    lax.fori_loop(0, cols // 2, join_grad, 0)

    summed = own[dp]
    for k in range(1, n_dp):
        d_copy(k).wait()
        summed = summed + dp_in[k].astype(F32)
    for z in range(nz):
        piece = summed[:, z * sub : (z + 1) * sub]
        if sub < 128:
            piece = jnp.concatenate([piece, jnp.zeros((half, 128 - sub), F32)], axis=1)
        shares[z] = piece
        z_out[z] = piece.astype(BF16)

    def z_copy(k):
        to = lax.rem(zi + k, nz)
        return remote(z_out.at[to], z_in.at[k], z_send.at[k], z_recv.at[k], dp, 2 * to + core)

    for k in range(1, nz):
        z_copy(k).start()
    summed = shares[zi]
    for k in range(1, nz):
        z_copy(k).wait()
        summed = summed + z_in[k].astype(F32)

    final[space] = summed.astype(BF16)

    def f_copy(k):
        return remote(final.at[space], final.at[space], f_send.at[k], f_recv.at[k], dp, lax.rem(space + k, n_space))

    for k in range(1, n_space):
        f_copy(k).start()
    for k in range(1, n_space):
        f_copy(k).wait()
    for z in range(nz):
        for c in range(2):
            total[c * half : (c + 1) * half, z * sub : (z + 1) * sub] = final[2 * z + c].astype(F32)[:, :sub]
    gradient = total[...].T[:shard, :C] / float(count)

    one = beta_one * moment_one[...] + (1.0 - beta_one) * gradient
    two = beta_two * moment_two[...] + (1.0 - beta_two) * gradient * gradient
    first_hat = one / (1.0 - beta_one**adam_step)
    second_hat = two / (1.0 - beta_two**adam_step)
    old = weight[...]
    new_one[...] = one
    new_two[...] = two
    new_weight[...] = old - learn_rate * (first_hat / (jnp.sqrt(second_hat) + epsilon) + decay_rate * old)


def body(n_dp, n_space, image, cotangent, weight, moment_one, moment_two):
    shard, C = weight.shape
    half = C // 2
    wide = up(shard, 128)
    rows = image.shape[1]
    out_rows = cotangent.shape[1]
    cols = cotangent.shape[2] // C
    positions = out_rows * cols
    nz = n_space // 2
    count = positions * n_dp * n_space
    vmem = pltpu.VMEM
    dma = pltpu.SemaphoreType.DMA
    spec = pl.BlockSpec(memory_space=pltpu.VMEM)
    return pl.pallas_call(
        functools.partial(kernel, n_dp, n_space, count),
        out_shape=(
            jax.ShapeDtypeStruct(cotangent.shape, BF16),
            jax.ShapeDtypeStruct(image.shape, BF16),
            jax.ShapeDtypeStruct(weight.shape, F32),
            jax.ShapeDtypeStruct(weight.shape, F32),
            jax.ShapeDtypeStruct(weight.shape, F32),
        ),
        in_specs=[spec] * 5,
        out_specs=[spec] * 5,
        scratch_shapes=[
            vmem((2, rows * cols + 24, 128), F32),
            vmem((2, rows * cols + 24, 128), F32),
            vmem((2, positions + 8, 128), F32),
            vmem((2, positions + 8, 128), F32),
            vmem((2 * cols, C), BF16),
            vmem((2 * cols, C), BF16),
            vmem((cols, C), BF16),
            vmem((cols, C), BF16),
            vmem((n_dp, 2, half, wide), BF16),
            vmem((9, positions, C), BF16),
            vmem((n_dp, half, wide), F32),
            vmem((n_dp, half, wide), BF16),
            vmem((n_dp, half, wide), BF16),
            vmem((n_dp, half, wide), F32),
            vmem((n_dp, half, wide), BF16),
            vmem((n_dp, half, wide), BF16),
            vmem((nz, half, 128), F32),
            vmem((nz, half, 128), BF16),
            vmem((nz, half, 128), BF16),
            vmem((n_space, half, 128), BF16),
            vmem((C, wide), F32),
            dma((2,)), dma((2,)),
            dma((n_dp,)), dma((n_dp,)), dma((n_dp,)), dma((n_dp,)),
            dma((1,)), dma((1,)),
            dma((n_dp,)), dma((n_dp,)),
            dma((nz,)), dma((nz,)),
            dma((n_space,)), dma((n_space,)),
        ],
        compiler_params=pltpu.CompilerParams(
            collective_id=0, has_side_effects=True, vmem_limit_bytes=48 * 1024 * 1024
        ),
    )(image, cotangent, weight, moment_one, moment_two)


def solution(mesh):
    whole = P("dp", "space", None)
    rows = P("dp", None)
    specs = (whole, whole, rows, rows, rows)
    return jax.shard_map(
        functools.partial(body, mesh.shape["dp"], mesh.shape["space"]),
        mesh=mesh, in_specs=specs, out_specs=specs, check_vma=False)
```

time: 132 us -> 32.3 us (0.24); the launches traced: 130 us -> 32.1 us
  blocking collectives: 47.2 us -> 0 us
  waiting for transfers between devices: 42.7 us -> 0 us
  Pallas kernels: 0 us -> 24.6 us
  between operations: 15.8 us -> 0.69 us
  local copies, waits for them, and re-layouts: 13.5 us -> 6.78 us
  starting transfers between devices: 6.27 us -> 0 us
  other arithmetic: 3.21 us -> 0 us
    unnamed x4 -> x0, waiting for transfers between devices: 41.9 us -> none
    pallas_call x0 -> x1, Pallas kernels: none -> 24.6 us  [body(): pl.pallas_call(functools.partial(kernel, n_dp, n_space, count), out_shape...]
    all_gather x2 -> x0, blocking collectives: 24.3 us -> none  [the longest x1 14.3 us: body(): grad_shard = lax.all_gather(by_owner, 'space', axis=1, tiled=True)]
    unnamed x1 -> x0, blocking collectives: 22.9 us -> none
    ppermute x2 -> x0, starting transfers between devices: 3.65 us -> none  [from_behind(): return lax.ppermute(block, axis, route)]
    slice x13 -> x0, local copies, waits for them, and re-layouts: 3.14 us -> none  [the longest x9 1.9 us: body(): padded[:, row_tap:row_tap + 2 * out_rows - 1:2, col_tap:col_tap + 2 * out...]
    reshape x5 -> x0, local copies, waits for them, and re-layouts: 3.13 us -> none  [the longest x1 1.23 us: body(): image_four = image.reshape(samples, rows_here, cols_here, channels)]
    unnamed x3 -> x0, starting transfers between devices: 2.62 us -> none
  transfers between devices with their start and end apart: 5 -> 0, of which waited for: 3 -> 0; matrix products, arithmetic and copies ran while one was open for 3% -> 0% of each run, Pallas kernels for 0% -> 0%
where the time goes in v1:
time: 32.3 us; the launch traced here: 32.1 us
  Pallas kernels  24.6 us (76%)
  local copies, waits for them, and re-layouts  6.78 us (21%)
  between operations  0.69 us (2%)
    pallas_call x1, Pallas kernels, body(): pl.pallas_call(functools.partial(kernel, n_dp, n_space, count), out_shape...  24.6 us
    unnamed x13, local copies, waits for them, and re-layouts  4.27 us
    pallas_call x3, local copies, waits for them, and re-layouts, body(): pl.pallas_call(functools.partial(kernel, n_dp, n_space, count), out_shape...  2.51 us

profile of v1, /device:TPU:0, one launch (start us, length us, event | category | flops | bytes accessed | tf_op | source)
XLA Modules:
  0.0 32.1 jit_solution(12243203600959315554)
XLA Ops:
  0.6 0.0 copy-start.2
  0.6 1.1 %copy.10.weight = f32[360,160]{1,0:T(8,128)S(1)} copy(f32[360,160]{0,1:T(8,128)} %param.7) | data formatting | bytes 460800 | tf_op args[2]
  1.8 0.0 copy-done.2
  1.8 0.0 copy-start.3
  1.8 0.2 copy.11.moment_one
  2.0 0.8 %copy-done.3 = f32[360,160]{0,1:T(8,128)S(1)} copy-done((f32[360,160]{0,1:T(8,128)S(1)}, f32[360,160]{0,1:T(8,128)}, u32[]{:S(2)}) %copy-start.3) | copy-done | bytes 230424
  2.7 0.0 copy-start
  2.8 0.0 copy-start.1
  2.8 0.2 copy.12.moment_two
  2.9 0.7 %copy-done = bf16[1,8,10240]{2,1,0:T(8,128)(2,1)S(1)} copy-done((bf16[1,8,10240]{2,1,0:T(8,128)(2,1)S(1)}, bf16[1,8,10240]{2,1,0:T(8,128)(2,1)}, u32[]{:S(2)}) %copy-start) | copy-done | bytes 163864
  3.7 0.0 copy-done.1
  3.7 24.6 %shard_map.92 = (bf16[1,4,5120]{2,1,0:T(4,128)(2,1)S(1)}, bf16[1,8,10240]{2,1,0:T(8,128)(2,1)S(1)}, f32[360,160]{1,0:T(8,128)S(1)}, f32[360,160]{1,0:T(8,128)S(1)}, f32[360,160]{1,0:T(8,128)S(1)}) custom-call(bf16[1,8,10240]{2,1,0:T(8,128)(2,1)S(1)} %copy-done, bf16[1,4,5120]{2,1,0:T(4,128)(2,1)S(1)} %copy-done.1, f32[360,160]{1,0:T(8,128)S(1)} %copy.10.weight, ...), custom_call_target="tpu_custom_call" | custom-call | tf_op jit(solution)/shard_map/pallas_call | solution.py:335
  28.3 0.8 %copy.13 = f32[360,160]{0,1:T(8,128)} copy(f32[360,160]{1,0:T(8,128)S(1)} %get-tuple-element.7) | data formatting | bytes 460800 | tf_op jit(solution)/shard_map/pallas_call | solution.py:335
  29.2 0.8 %copy.14 = f32[360,160]{0,1:T(8,128)} copy(f32[360,160]{1,0:T(8,128)S(1)} %get-tuple-element.8) | data formatting | bytes 460800 | tf_op jit(solution)/shard_map/pallas_call | solution.py:335
  30.0 0.8 %copy.15 = f32[360,160]{0,1:T(8,128)} copy(f32[360,160]{1,0:T(8,128)S(1)} %get-tuple-element.9) | data formatting | bytes 460800 | tf_op jit(solution)/shard_map/pallas_call | solution.py:335
  30.8 0.6 %copy.18 = bf16[1,4,5120]{2,1,0:T(4,128)(2,1)} copy(bf16[1,4,5120]{2,1,0:T(4,128)(2,1)S(1)} %get-tuple-element.15) | data formatting | bytes 81920
  31.4 0.7 %copy.19 = bf16[1,8,10240]{2,1,0:T(8,128)(2,1)} copy(bf16[1,8,10240]{2,1,0:T(8,128)(2,1)S(1)} %get-tuple-element.16) | data formatting | bytes 327680
Async XLA Ops:
  0.6 1.2 %copy-start.2 = (f32[360,160]{0,1:T(8,128)S(1)}, f32[360,160]{0,1:T(8,128)}, u32[]{:S(2)}) copy-start(f32[360,160]{0,1:T(8,128)} %param.8) | copy-start | bytes 691204
  1.8 0.9 %copy-start.3 = (f32[360,160]{0,1:T(8,128)S(1)}, f32[360,160]{0,1:T(8,128)}, u32[]{:S(2)}) copy-start(f32[360,160]{0,1:T(8,128)} %param.9) | copy-start | bytes 691204
  2.7 0.9 %copy-start = (bf16[1,8,10240]{2,1,0:T(8,128)(2,1)S(1)}, bf16[1,8,10240]{2,1,0:T(8,128)(2,1)}, u32[]{:S(2)}) copy-start(bf16[1,8,10240]{2,1,0:T(8,128)(2,1)} %image.1) | copy-start | bytes 491524
  2.8 0.9 %copy-start.1 = (bf16[1,4,5120]{2,1,0:T(4,128)(2,1)S(1)}, bf16[1,4,5120]{2,1,0:T(4,128)(2,1)}, u32[]{:S(2)}) copy-start(bf16[1,4,5120]{2,1,0:T(4,128)(2,1)} %cotangent.1) | copy-start | bytes 122884

commit v2 on v1

--- a/solution.py
+++ b/solution.py
@@ -24,30 +24,34 @@
 
 
 def kernel(
-    n_dp, n_space, count,
-    image, cotangent, weight, moment_one, moment_two,
-    out, grad_image, new_weight, new_one, new_two,
-    even, odd, cot, cot_next, img_edge_out, img_edge_in, cot_edge_out, cot_edge_in,
-    wt, taps, part, mate_out, mate_in, own, dp_out, dp_in, shares, z_out, z_in, final, total,
-    edge_send, edge_recv, w_send, w_recv, wm_send, wm_recv, m_send, m_recv,
+    n_dp, n_space,
+    image_hbm, cotangent_hbm, weight_hbm, one_hbm, two_hbm,
+    out, grad_image, gradient, weight, one, two,
+    image, cotangent, kern, even, odd, cot, cot_next, img_edge_out, img_edge_in, cot_edge_out, cot_edge_in,
+    wt, taps, part, mate_out, mate_in, own, dp_out, dp_in, shares, z_out, z_in, final,
+    load,    edge_send, edge_recv, w_send, w_recv, wm_send, wm_recv, m_send, m_recv,
     d_send, d_recv, z_send, z_recv, f_send, f_recv,
 ):
-    C = weight.shape[1]
+    C, shard = weight.shape
     half = C // 2
     rest = C - 128
-    shard = weight.shape[0]
     wide = wt.shape[-1]
     cols = out.shape[2] // C
     out_rows = out.shape[1]
     rows = image.shape[1]
     positions = cols * out_rows
     nz = n_space // 2
-    sub = wide // nz
+    blocks = wide // 128
     dp = lax.axis_index("dp")
     space = lax.axis_index("space")
     core = lax.rem(space, 2)
     zi = lax.div(space, 2)
     mate = space + 1 - 2 * core
+
+    loads = [pltpu.make_async_copy(src, dst, load.at[n]) for n, (src, dst) in enumerate(
+        ((cotangent_hbm, cotangent), (image_hbm, image), (weight_hbm, weight), (one_hbm, one), (two_hbm, two)))]
+    for copy in loads:
+        copy.start()
 
     barrier = pltpu.get_barrier_semaphore()
     for k in range(1, n_dp):
@@ -81,6 +85,7 @@
             cot[1, pl.ds(at, 8), 0:rest] = both[:, 128:]
         return carry
 
+    loads[0].wait()
     lax.fori_loop(0, cols // 4, split_cot, 0)
 
     def split_image(g, carry):
@@ -93,6 +98,7 @@
             ref[1, pl.ds(at, rows), 0:rest] = piece[:, 128:]
         return carry
 
+    loads[1].wait()
     lax.fori_loop(0, cols // 2, split_image, 0)
 
     def strided(ref, start, size, stride):
@@ -103,10 +109,8 @@
     img_edge_out[cols : 2 * cols] = strided(odd, 16 + rows - 1, cols, rows).astype(BF16)
     cot_edge_out[...] = strided(cot, 0, cols, out_rows).astype(BF16)
 
-    eye = (lax.broadcasted_iota(jnp.int32, (C, C), 0) == lax.broadcasted_iota(jnp.int32, (C, C), 1))
-    eye = eye.astype(F32).astype(BF16)
-    mine = lax.dot_general(eye, weight[...].astype(BF16), (((1,), (1,)), ((), ())),
-                           preferred_element_type=F32).astype(BF16)
+    loads[2].wait()
+    mine = weight[...].astype(BF16)
     wt[dp, 0, :, 0:shard] = mine[:half]
     wt[dp, 1, :, 0:shard] = mine[half:]
 
@@ -115,8 +119,13 @@
     img_copy = remote(img_edge_out, img_edge_in, edge_send.at[0], edge_recv.at[0], dp, lax.rem(space + 1, n_space))
     cot_copy = remote(cot_edge_out, cot_edge_in, edge_send.at[1], edge_recv.at[1], dp, lax.rem(space + n_space - 1, n_space))
 
-    img_copy.start()
-    cot_copy.start()
+    @pl.when(space < n_space - 1)
+    def _():
+        img_copy.start()
+
+    @pl.when(space > 0)
+    def _():
+        cot_copy.start()
 
     def w_copy(k):
         return remote(wt.at[dp, core], wt.at[dp, core], w_send.at[k], w_recv.at[k], lax.rem(dp + k, n_dp), space)
@@ -159,7 +168,22 @@
 
     grads(1)
     grads(2)
-    img_copy.wait()
+    cut = -(-3 * C // shard)
+
+    def mate_copy(n):
+        at = pl.ds(0, cut) if n else pl.ds(cut, n_dp - cut)
+        return remote(mate_out.at[at], mate_in.at[at], m_send.at[n], m_recv.at[n], dp, mate)
+
+    mate_out[cut:] = part[cut:].astype(BF16)
+    mate_copy(0).start()
+
+    @pl.when(space < n_space - 1)
+    def _():
+        img_copy.wait_send()
+
+    @pl.when(space > 0)
+    def _():
+        img_copy.wait_recv()
 
     @pl.when(space == 0)
     def _():
@@ -171,22 +195,18 @@
         ref[0, at, :] = edge[:, :128]
         ref[1, at, :] = jnp.concatenate([edge[:, 128:], jnp.zeros((cols, 256 - C), F32)], axis=1)
     grads(0)
-    mate_out[...] = part[...].astype(BF16)
-    mate_copy = remote(mate_out, mate_in, m_send.at[0], m_recv.at[0], dp, mate)
-    mate_copy.start()
+    mate_out[:cut] = part[:cut].astype(BF16)
+    mate_copy(1).start()
 
     def wm_copy(k):
         src = lax.rem(dp + n_dp - k, n_dp)
         return remote(wt.at[src, core], wt.at[src, core], wm_send.at[k], wm_recv.at[k], dp, mate)
 
-    for k in range(1, n_dp):
-        w_copy(k).wait()
-        wm_copy(k).start()
-
-    for t in range(9):
+    for t in (3, 4, 5, 6, 7, 8, 0, 1, 2):
         place(own, t, jnp.dot(own_rows, taps[t], preferred_element_type=F32), True)
 
-    mate_copy.wait()
+    mate_copy(0).wait()
+    mate_copy(1).wait()
     own[...] = own[...] + mate_in[...].astype(F32)
 
     dp_out[...] = own[...].astype(BF16)
@@ -198,6 +218,31 @@
     for k in range(1, n_dp):
         d_copy(k).start()
 
+    for k in range(1, n_dp):
+        w_copy(k).wait()
+        wm_copy(k).start()
+
+    def keep(ref, at, value):
+        ref[0, at, :] = value[:, :128]
+        ref[1, at, :] = jnp.concatenate([value[:, 128:], jnp.zeros((value.shape[0], 256 - C), F32)], axis=1)
+
+    @pl.when(space > 0)
+    def _():
+        cot_copy.wait_send()
+
+    @pl.when(space < n_space - 1)
+    def _():
+        cot_copy.wait_recv()
+
+    @pl.when(space == n_space - 1)
+    def _():
+        cot_edge_in[...] = jnp.zeros(cot_edge_in.shape, BF16)
+
+    for h in range(2):
+        cot_next[h, pl.ds(0, positions), :] = cot[h, pl.ds(1, positions), :]
+    edge = cot_edge_in[...].astype(F32)
+    at = pl.ds(out_rows - 1, cols, stride=out_rows)
+    keep(cot_next, at, edge)
     for k in range(1, n_dp):
         wm_copy(k).wait()
 
@@ -214,15 +259,11 @@
         value = pieces[0] if len(pieces) == 1 else jnp.concatenate(pieces, axis=1)
         return value.astype(BF16)
 
-    kern = [tap_t(t) for t in range(9)]
+    for t in range(9):
+        kern[t] = tap_t(t)
     acc = jnp.zeros((positions, C), F32)
     for t in range(9):
         acc = acc + lax.dot_general(taps[t], kern[t], (((1,), (1,)), ((), ())), preferred_element_type=F32)
-    total_shape = total.shape
-
-    def keep(ref, at, value):
-        ref[0, at, :] = value[:, :128]
-        ref[1, at, :] = jnp.concatenate([value[:, 128:], jnp.zeros((value.shape[0], 256 - C), F32)], axis=1)
 
     keep(even, pl.ds(0, positions), acc)
 
@@ -237,17 +278,24 @@
 
     lax.fori_loop(0, cols // 4, join_out, 0)
 
-    cot_copy.wait()
-
-    @pl.when(space == n_space - 1)
-    def _():
-        cot_edge_in[...] = jnp.zeros(cot_edge_in.shape, BF16)
-
-    for h in range(2):
-        cot_next[h, pl.ds(0, positions), :] = cot[h, pl.ds(1, positions), :]
-    edge = cot_edge_in[...].astype(F32)
-    at = pl.ds(out_rows - 1, cols, stride=out_rows)
-    keep(cot_next, at, edge)
+    summed = own[dp]
+    for k in range(1, n_dp):
+        d_copy(k).wait()
+        summed = summed + dp_in[k].astype(F32)
+    pieces = [summed[:, b * 128 : (b + 1) * 128] for b in range(blocks)]
+    height = blocks * half
+    if nz * shares.shape[1] > height:
+        pieces.append(jnp.zeros((nz * shares.shape[1] - height, 128), F32))
+    stacked = jnp.concatenate(pieces, axis=0).reshape(shares.shape)
+    shares[...] = stacked
+    z_out[...] = stacked.astype(BF16)
+
+    def z_copy(k):
+        to = lax.rem(zi + k, nz)
+        return remote(z_out.at[to], z_in.at[k], z_send.at[k], z_recv.at[k], dp, 2 * to + core)
+
+    for k in range(1, nz):
+        z_copy(k).start()
     here = whole_cot.astype(BF16)
     right = strided(cot, out_rows, positions, 1).astype(BF16)
     below = strided(cot_next, 0, positions, 1).astype(BF16)
@@ -258,6 +306,18 @@
 
     keep(even, pl.ds(0, positions, stride=2), back(here, 1, 1))
     keep(even, pl.ds(1, positions, stride=2), back(here, 2, 1) + back(below, 0, 1))
+    summed = shares[zi]
+    for k in range(1, nz):
+        z_copy(k).wait()
+        summed = summed + z_in[k].astype(F32)
+
+    final[space] = summed.astype(BF16)
+
+    def f_copy(k):
+        return remote(final.at[space], final.at[space], f_send.at[k], f_recv.at[k], dp, lax.rem(space + k, n_space))
+
+    for k in range(1, n_space):
+        f_copy(k).start()
     keep(odd, pl.ds(0, positions, stride=2), back(here, 1, 2) + back(right, 1, 0))
     keep(odd, pl.ds(1, positions, stride=2),
          back(here, 2, 2) + back(right, 2, 0) + back(below, 0, 2) + back(both, 0, 0))
@@ -273,50 +333,43 @@
 
     lax.fori_loop(0, cols // 2, join_grad, 0)
 
-    summed = own[dp]
-    for k in range(1, n_dp):
-        d_copy(k).wait()
-        summed = summed + dp_in[k].astype(F32)
-    for z in range(nz):
-        piece = summed[:, z * sub : (z + 1) * sub]
-        if sub < 128:
-            piece = jnp.concatenate([piece, jnp.zeros((half, 128 - sub), F32)], axis=1)
-        shares[z] = piece
-        z_out[z] = piece.astype(BF16)
-
-    def z_copy(k):
-        to = lax.rem(zi + k, nz)
-        return remote(z_out.at[to], z_in.at[k], z_send.at[k], z_recv.at[k], dp, 2 * to + core)
-
-    for k in range(1, nz):
-        z_copy(k).start()
-    summed = shares[zi]
-    for k in range(1, nz):
-        z_copy(k).wait()
-        summed = summed + z_in[k].astype(F32)
-
-    final[space] = summed.astype(BF16)
-
-    def f_copy(k):
-        return remote(final.at[space], final.at[space], f_send.at[k], f_recv.at[k], dp, lax.rem(space + k, n_space))
-
-    for k in range(1, n_space):
-        f_copy(k).start()
     for k in range(1, n_space):
         f_copy(k).wait()
-    for z in range(nz):
-        for c in range(2):
-            total[c * half : (c + 1) * half, z * sub : (z + 1) * sub] = final[2 * z + c].astype(F32)[:, :sub]
-    gradient = total[...].T[:shard, :C] / float(count)
-
-    one = beta_one * moment_one[...] + (1.0 - beta_one) * gradient
-    two = beta_two * moment_two[...] + (1.0 - beta_two) * gradient * gradient
+    gradient[...] = final[...]
+    loads[3].wait()
+    loads[4].wait()
+
+
+def finish(count, out_in, grad_in, gradient, weight, moment_one, moment_two,
+           out, grad_image, new_weight, new_one, new_two, w_buf, one_buf, two_buf, sems):
+    C, shard = weight.shape
+    half = C // 2
+    copies = [pltpu.make_async_copy(out_in, out, sems.at[0]),
+              pltpu.make_async_copy(grad_in, grad_image, sems.at[1])]
+    for copy in copies:
+        copy.start()
+    blocks = up(shard, 128) // 128
+    halves = []
+    for c in range(2):
+        stacked = jnp.concatenate([gradient[n].astype(F32) for n in range(c, gradient.shape[0], 2)], axis=0)
+        halves.append(jnp.concatenate([stacked[b * half : (b + 1) * half] for b in range(blocks)], axis=1))
+    grad = jnp.concatenate(halves, axis=0)[:, :shard] / float(count)
+    one = beta_one * moment_one[...] + (1.0 - beta_one) * grad
+    one_buf[...] = one
+    copies.append(pltpu.make_async_copy(one_buf, new_one, sems.at[2]))
+    copies[-1].start()
+    two = beta_two * moment_two[...] + (1.0 - beta_two) * grad * grad
+    two_buf[...] = two
+    copies.append(pltpu.make_async_copy(two_buf, new_two, sems.at[3]))
+    copies[-1].start()
     first_hat = one / (1.0 - beta_one**adam_step)
     second_hat = two / (1.0 - beta_two**adam_step)
     old = weight[...]
-    new_one[...] = one
-    new_two[...] = two
-    new_weight[...] = old - learn_rate * (first_hat / (jnp.sqrt(second_hat) + epsilon) + decay_rate * old)
+    w_buf[...] = old - learn_rate * (first_hat / (jnp.sqrt(second_hat) + epsilon) + decay_rate * old)
+    copies.append(pltpu.make_async_copy(w_buf, new_weight, sems.at[4]))
+    copies[-1].start()
+    for copy in copies:
+        copy.wait()
 
 
 def body(n_dp, n_space, image, cotangent, weight, moment_one, moment_two):
@@ -332,18 +385,24 @@
     vmem = pltpu.VMEM
     dma = pltpu.SemaphoreType.DMA
     spec = pl.BlockSpec(memory_space=pltpu.VMEM)
-    return pl.pallas_call(
-        functools.partial(kernel, n_dp, n_space, count),
+    hbm = pl.BlockSpec(memory_space=pltpu.HBM)
+    share = up(up(wide * half // 128, nz) // nz, 16)
+    weight_t = weight.T
+    state = jax.ShapeDtypeStruct(weight_t.shape, F32)
+    out, grad_image, gradient, *held = pl.pallas_call(
+        functools.partial(kernel, n_dp, n_space),
         out_shape=(
             jax.ShapeDtypeStruct(cotangent.shape, BF16),
             jax.ShapeDtypeStruct(image.shape, BF16),
-            jax.ShapeDtypeStruct(weight.shape, F32),
-            jax.ShapeDtypeStruct(weight.shape, F32),
-            jax.ShapeDtypeStruct(weight.shape, F32),
+            jax.ShapeDtypeStruct((n_space, share, 128), BF16),
+            state, state, state,
         ),
-        in_specs=[spec] * 5,
-        out_specs=[spec] * 5,
+        in_specs=[hbm] * 5,
+        out_specs=[spec] * 6,
         scratch_shapes=[
+            vmem(image.shape, BF16),
+            vmem(cotangent.shape, BF16),
+            vmem((9, C, C), BF16),
             vmem((2, rows * cols + 24, 128), F32),
             vmem((2, rows * cols + 24, 128), F32),
             vmem((2, positions + 8, 128), F32),
@@ -360,22 +419,35 @@
             vmem((n_dp, half, wide), F32),
             vmem((n_dp, half, wide), BF16),
             vmem((n_dp, half, wide), BF16),
-            vmem((nz, half, 128), F32),
-            vmem((nz, half, 128), BF16),
-            vmem((nz, half, 128), BF16),
-            vmem((n_space, half, 128), BF16),
-            vmem((C, wide), F32),
+            vmem((nz, share, 128), F32),
+            vmem((nz, share, 128), BF16),
+            vmem((nz, share, 128), BF16),
+            vmem((n_space, share, 128), BF16),
+            dma((5,)),
             dma((2,)), dma((2,)),
             dma((n_dp,)), dma((n_dp,)), dma((n_dp,)), dma((n_dp,)),
-            dma((1,)), dma((1,)),
+            dma((2,)), dma((2,)),
             dma((n_dp,)), dma((n_dp,)),
             dma((nz,)), dma((nz,)),
             dma((n_space,)), dma((n_space,)),
         ],
         compiler_params=pltpu.CompilerParams(
-            collective_id=0, has_side_effects=True, vmem_limit_bytes=48 * 1024 * 1024
+            collective_id=0, has_side_effects=True, vmem_limit_bytes=24 * 1024 * 1024
         ),
-    )(image, cotangent, weight, moment_one, moment_two)
+    )(image, cotangent, weight_t, moment_one.T, moment_two.T)
+    out, grad_image, new_weight, new_one, new_two = pl.pallas_call(
+        functools.partial(finish, count),
+        out_shape=(
+            jax.ShapeDtypeStruct(cotangent.shape, BF16),
+            jax.ShapeDtypeStruct(image.shape, BF16),
+            state, state, state,
+        ),
+        in_specs=[spec] * 6,
+        out_specs=[hbm] * 5,
+        scratch_shapes=[vmem(weight_t.shape, F32)] * 3 + [dma((5,))],
+        compiler_params=pltpu.CompilerParams(vmem_limit_bytes=16 * 1024 * 1024),
+    )(out, grad_image, gradient, *held)
+    return out, grad_image, new_weight.T, new_one.T, new_two.T
 
 
 def solution(mesh):

time: 32.3 us -> 29.5 us (0.913)
  local copies, waits for them, and re-layouts: 6.78 us -> 4.52 us
  Pallas kernels: 24.6 us -> 24.1 us
    pallas_call x3 -> x0, local copies, waits for them, and re-layouts: 2.51 us -> none  [body(): pl.pallas_call(functools.partial(kernel, n_dp, n_space, count), out_shape...]
    pallas_call x1 -> x2, Pallas kernels: 24.6 us -> 24.1 us  [the longest x1 23.1 us: body(): pl.pallas_call(functools.partial(kernel, n_dp, n_space), out_shape=(jax.S...]
    unnamed x13 -> x10, local copies, waits for them, and re-layouts: 4.27 us -> 4.52 us
where the time goes in v2:
time: 29.5 us; the launch traced here: 29.3 us
  Pallas kernels  24.1 us (82%)
  local copies, waits for them, and re-layouts  4.52 us (15%)
  between operations  0.65 us (2%)
    pallas_call x1, Pallas kernels, body(): pl.pallas_call(functools.partial(kernel, n_dp, n_space), out_shape=(jax.S...  23.1 us
    unnamed x10, local copies, waits for them, and re-layouts  4.52 us
    pallas_call x1, Pallas kernels, body(): pl.pallas_call(functools.partial(finish, count), out_shape=(jax.ShapeDtyp...  1.01 us

profile of v2, /device:TPU:0, one launch (start us, length us, event | category | flops | bytes accessed | tf_op | source)
XLA Modules:
  0.0 29.3 jit_solution(18072183722094923102)
XLA Ops:
  0.6 0.0 copy-start
  0.6 0.9 %copy-done = f32[360,160]{0,1:T(8,128)S(1)} copy-done((f32[360,160]{0,1:T(8,128)S(1)}, f32[360,160]{0,1:T(8,128)}, u32[]{:S(2)}) %copy-start) | copy-done | bytes 230424
  1.6 0.0 copy-start.1
  1.6 0.9 %copy-done.1 = f32[360,160]{0,1:T(8,128)S(1)} copy-done((f32[360,160]{0,1:T(8,128)S(1)}, f32[360,160]{0,1:T(8,128)}, u32[]{:S(2)}) %copy-start.1) | copy-done | bytes 230424
  2.5 0.0 copy-start.2
  2.5 0.9 %copy-done.2 = f32[360,160]{0,1:T(8,128)S(1)} copy-done((f32[360,160]{0,1:T(8,128)S(1)}, f32[360,160]{0,1:T(8,128)}, u32[]{:S(2)}) %copy-start.2) | copy-done | bytes 230424
  3.5 0.0 copy-start.3
  3.5 0.9 %copy-done.3 = bf16[1,8,10240]{2,1,0:T(8,128)(2,1)S(1)} copy-done((bf16[1,8,10240]{2,1,0:T(8,128)(2,1)S(1)}, bf16[1,8,10240]{2,1,0:T(8,128)(2,1)}, u32[]{:S(2)}) %copy-start.3) | copy-done | bytes 163864
  4.4 0.0 copy-start.4
  4.4 0.8 %copy-done.4 = bf16[1,4,5120]{2,1,0:T(4,128)(2,1)S(1)} copy-done((bf16[1,4,5120]{2,1,0:T(4,128)(2,1)S(1)}, bf16[1,4,5120]{2,1,0:T(4,128)(2,1)}, u32[]{:S(2)}) %copy-start.4) | copy-done | bytes 40984
  5.2 23.1 %shard_map.92 = (bf16[1,4,5120]{2,1,0:T(4,128)(2,1)S(1)}, bf16[1,8,10240]{2,1,0:T(8,128)(2,1)S(1)}, bf16[8,64,128]{2,1,0:T(8,128)(2,1)S(1)}, f32[160,360]{1,0:T(...) custom-call(bf16[1,8,10240]{2,1,0:T(8,128)(2,1)S(1)} %copy-done.3, bf16[1,4,5120]{2,1,0:T(4,128)(2,1)S(1)} %copy-done.4, ...), custom_call_target="tpu_custom_call" | custom-call | tf_op jit(solution)/shard_map/pallas_call | solution.py:392
  28.2 1.0 %shard_map.93 = (bf16[1,4,5120]{2,1,0:T(4,128)(2,1)}, bf16[1,8,10240]{2,1,0:T(8,128)(2,1)}, f32[160,360]{1,0:T(8,128)}, f32[160,360]{1,0:T(8,128)}, f32[160,360]{1,0:T(8,128)}) custom-call(bf16[1,4,5120]{2,1,0:T(4,128)(2,1)S(1)} %get-tuple-element.16.out_in, bf16[1,8,10240]{2,1,0:T(8,128)(2,1)S(1)} %get-tuple-element.17.grad_in, ...), custom_call_target="tpu_custom_call" | custom-call | tf_op jit(solution)/shard_map/pallas_call | solution.py:438
Async XLA Ops:
  0.6 0.9 %copy-start = (f32[360,160]{0,1:T(8,128)S(1)}, f32[360,160]{0,1:T(8,128)}, u32[]{:S(2)}) copy-start(f32[360,160]{0,1:T(8,128)} %param.7) | copy-start | bytes 691204
  1.6 0.9 %copy-start.1 = (f32[360,160]{0,1:T(8,128)S(1)}, f32[360,160]{0,1:T(8,128)}, u32[]{:S(2)}) copy-start(f32[360,160]{0,1:T(8,128)} %param.8) | copy-start | bytes 691204
  2.5 0.9 %copy-start.2 = (f32[360,160]{0,1:T(8,128)S(1)}, f32[360,160]{0,1:T(8,128)}, u32[]{:S(2)}) copy-start(f32[360,160]{0,1:T(8,128)} %param.9) | copy-start | bytes 691204
  3.5 0.9 %copy-start.3 = (bf16[1,8,10240]{2,1,0:T(8,128)(2,1)S(1)}, bf16[1,8,10240]{2,1,0:T(8,128)(2,1)}, u32[]{:S(2)}) copy-start(bf16[1,8,10240]{2,1,0:T(8,128)(2,1)} %image_hbm.1) | copy-start | bytes 491524
  4.4 0.8 %copy-start.4 = (bf16[1,4,5120]{2,1,0:T(4,128)(2,1)S(1)}, bf16[1,4,5120]{2,1,0:T(4,128)(2,1)}, u32[]{:S(2)}) copy-start(bf16[1,4,5120]{2,1,0:T(4,128)(2,1)} %cotangent_hbm.1) | copy-start | bytes 122884

commit v3 on v2

--- a/solution.py
+++ b/solution.py
@@ -434,7 +434,8 @@
         compiler_params=pltpu.CompilerParams(
             collective_id=0, has_side_effects=True, vmem_limit_bytes=24 * 1024 * 1024
         ),
-    )(image, cotangent, weight_t, moment_one.T, moment_two.T)
+    )(*(pltpu.with_memory_space_constraint(x, pltpu.HBM)
+        for x in (image, cotangent, weight_t, moment_one.T, moment_two.T)))
     out, grad_image, new_weight, new_one, new_two = pl.pallas_call(
         functools.partial(finish, count),
         out_shape=(

time: 29.5 us -> 23.8 us (0.81)
  local copies, waits for them, and re-layouts: 4.52 us -> 0 us
  Pallas kernels: 24.1 us -> 23 us
    unnamed x10 -> x0, local copies, waits for them, and re-layouts: 4.52 us -> none
    pallas_call x1, Pallas kernels: 23.1 us -> 22 us  [body(): pl.pallas_call(functools.partial(kernel, n_dp, n_space), out_shape=(jax.S...]
where the time goes in v3:
time: 23.8 us; the launch traced here: 23.6 us
  Pallas kernels  23 us (97%)
  between operations  0.64 us (3%)
    pallas_call x1, Pallas kernels, body(): pl.pallas_call(functools.partial(kernel, n_dp, n_space), out_shape=(jax.S...  22 us
    pallas_call x1, Pallas kernels, body(): pl.pallas_call(functools.partial(finish, count), out_shape=(jax.ShapeDtyp...  1.01 us

profile of v3, /device:TPU:0, one launch (start us, length us, event | category | flops | bytes accessed | tf_op | source)
XLA Modules:
  0.0 23.6 jit_solution(1669108084091348604)
XLA Ops:
  0.6 22.0 %shard_map.92 = (bf16[1,4,5120]{2,1,0:T(4,128)(2,1)S(1)}, bf16[1,8,10240]{2,1,0:T(8,128)(2,1)S(1)}, bf16[8,64,128]{2,1,0:T(8,128)(2,1)S(1)}, f32[160,360]{1,0:T(...) custom-call(bf16[1,8,10240]{2,1,0:T(8,128)(2,1)} %image_hbm.1, bf16[1,4,5120]{2,1,0:T(4,128)(2,1)} %cotangent_hbm.1, ...), custom_call_target="tpu_custom_call" | custom-call | tf_op jit(solution)/shard_map/pallas_call | solution.py:392
  22.6 1.0 %shard_map.93 = (bf16[1,4,5120]{2,1,0:T(4,128)(2,1)}, bf16[1,8,10240]{2,1,0:T(8,128)(2,1)}, f32[160,360]{1,0:T(8,128)}, f32[160,360]{1,0:T(8,128)}, f32[160,360]{1,0:T(8,128)}) custom-call(bf16[1,4,5120]{2,1,0:T(4,128)(2,1)S(1)} %get-tuple-element.16.out_in, bf16[1,8,10240]{2,1,0:T(8,128)(2,1)S(1)} %get-tuple-element.17.grad_in, ...), custom_call_target="tpu_custom_call" | custom-call | tf_op jit(solution)/shard_map/pallas_call | solution.py:439
